TPU v7x, 256 devices: a whole 4x4x8 slice. The times are simulated.
256 devices in a mesh: ctx: 32 (over z, y), ep: 8 (over x, core).
Axes of the slice: x: 4, y: 4, z: 8, core: 2. Of those that a mesh axis runs over, the one named last changes fastest.
Arguments:
- tokens: bfloat16 [8, 8192, 2048], P('ep', 'ctx'), may hold values from -12 to 12
- queries: bfloat16 [8, 8192, 2048], P('ep', 'ctx'), may hold values from -100 to 100
- keys: bfloat16 [8, 8192, 256], P('ep', 'ctx'), may hold values from -4 to 4
- values: bfloat16 [8, 8192, 256], P('ep', 'ctx'), may hold values from -6 to 6
- lengths: int32 [8, 16], P('ep'), may hold values from 1 to 2048, 8192 in all within a row
- out_proj: bfloat16 [2048, 2048], P('ctx'), may hold values from -0.5 to 0.5
- norm_gain: float32 [2048], replicated, may hold values from 0.5 to 1.5
- expert_ids: int32 [8, 8192, 1], P('ep', 'ctx'), may hold values from 0 to 7; in each aligned block of 256 rows (0 to 255, 256 to 511, ..., all dimensions but the last counted through in order) at most 64 rows name the same one
- gate_prob: float32 [8, 8192, 1], P('ep', 'ctx'), may hold values from 0.2 to 1
- w_gate: bfloat16 [8, 2048, 768], P('ep'), may hold values from -0.125 to 0.125
- w_up: bfloat16 [8, 2048, 768], P('ep'), may hold values from -0.125 to 0.125
- w_down: bfloat16 [8, 768, 2048], P('ep'), may hold values from -0.21875 to 0.21875
Outputs:
- layer_out: bfloat16 [8, 8192, 2048], P('ep', 'ctx')
Inputs may be any that keep to these rules, and one draw needn't show every extreme that they name: Each sequence's 16 lengths sum to 8192; the longest is exactly 2048. `expert_ids`: among the 256 tokens of one device at most 64 name the same expert, and in every draw some device has an expert named by exactly 64 of its tokens.
All inputs are finite; a program needn't handle non-finite values.
Results may differ from a plain program's by a relative error of at most 0.015.
Values may be sent and summed in bfloat16 or wider, within the bound.
No kernel may reach another device: no remote copies, remote signals or barrier semaphores. Data moves between devices by JAX's collectives and lax.ppermute only.
A program may use at most 128 MiB of HBM per device.

v0:
```python
import math

import jax
import jax.numpy as jnp
from jax import lax
from jax.sharding import PartitionSpec as P

HEAD_SIZE = 128
CAP = 64


masked_value = -1e30
norm_epsilon = 1e-06


def from_behind(array, axis, by):
    peers = lax.axis_size(axis)
    pairs = [(i, i + by) for i in range(peers) if 0 <= i + by < peers]
    return lax.ppermute(array, axis, pairs)


def on_device(
    tokens,
    queries,
    keys,
    values,
    lengths,
    out_proj,
    norm_gain,
    expert_ids,
    gate_prob,
    w_gate,
    w_up,
    w_down,
):
    tok_rows = tokens.shape[1]
    width = tokens.shape[2]
    head_count = queries.shape[2] // HEAD_SIZE
    kv_heads = keys.shape[2] // HEAD_SIZE
    query_group_size = head_count // kv_heads
    score_scale = 1.0 / math.sqrt(HEAD_SIZE)
    cycle_size = lax.axis_size("ctx")
    own_index = lax.axis_index("ctx")
    bounds = jnp.cumsum(lengths[0], dtype=jnp.int32)

    def document_ids(positions):
        return jnp.sum(
            (positions[:, None] >= bounds[None, :]).astype(jnp.int32), axis=1, dtype=jnp.int32
        )

    offsets = jnp.arange(tok_rows, dtype=jnp.int32)
    own_pos = own_index * tok_rows + offsets
    own_doc = document_ids(own_pos)
    query_grid = queries[0].reshape(tok_rows, kv_heads, query_group_size, HEAD_SIZE)

    def absorb(state, key_tile_block, value_tile_block, source):
        key_pos = source * tok_rows + offsets
        visible = (document_ids(key_pos)[None, :] == own_doc[:, None]) & (
            key_pos[None, :] <= own_pos[:, None]
        )
        visible = visible & (key_pos[None, :] >= 0)

        def update(carry):
            run_max, run_sum, run_acc = carry
            scores = (
                jnp.einsum(
                    "qhgd,khd->hgqk",
                    query_grid,
                    key_tile_block.reshape(tok_rows, kv_heads, HEAD_SIZE),
                    preferred_element_type=jnp.float32,
                )
                * score_scale
            )
            scores = jnp.where(visible[None, None], scores, masked_value)
            new_max = jnp.maximum(run_max, jnp.max(scores, axis=-1))
            factor = jnp.exp(run_max - new_max)
            weights = jnp.exp(scores - new_max[..., None])
            new_sum = run_sum * factor + jnp.sum(weights, axis=-1)
            mixed = jnp.einsum(
                "hgqk,khd->hgqd",
                weights.astype(jnp.bfloat16),
                value_tile_block.reshape(tok_rows, kv_heads, HEAD_SIZE),
                preferred_element_type=jnp.float32,
            )
            return (new_max, new_sum, run_acc * factor[..., None] + mixed)

        return lax.cond(jnp.any(visible), update, lambda carry: carry, state)

    start_state = (
        jnp.full((kv_heads, query_group_size, tok_rows), masked_value, jnp.float32),
        jnp.zeros((kv_heads, query_group_size, tok_rows), jnp.float32),
        jnp.zeros((kv_heads, query_group_size, tok_rows, HEAD_SIZE), jnp.float32),
    )
    state = absorb(start_state, keys[0], values[0], own_index)

    def circle(turn, carry):
        key_tile_block, value_tile_block, inner = carry
        key_tile_block, value_tile_block = from_behind((key_tile_block, value_tile_block), "ctx", 1)
        return (
            key_tile_block,
            value_tile_block,
            absorb(inner, key_tile_block, value_tile_block, own_index - turn),
        )

    final = lax.fori_loop(1, cycle_size, circle, (keys[0], values[0], state))
    run_max, run_sum, run_acc = final[2]
    attention = (
        (run_acc / run_sum[..., None])
        .transpose(2, 0, 1, 3)
        .reshape(tok_rows, width)
        .astype(jnp.bfloat16)
    )
    projected = jnp.dot(
        attention,
        lax.all_gather(out_proj, "ctx", axis=0, tiled=True),
        preferred_element_type=jnp.float32,
    )
    residual = (tokens[0].astype(jnp.float32) + projected).astype(jnp.bfloat16)
    residual_wide = residual.astype(jnp.float32)
    normed = residual_wide * lax.rsqrt(
        jnp.mean(residual_wide * residual_wide, axis=-1, keepdims=True) + norm_epsilon
    )
    normed = (normed * norm_gain).astype(jnp.bfloat16)
    group_devices = lax.axis_size("ep")
    local_experts = w_gate.shape[0]
    experts_in = local_experts * group_devices
    chosen = expert_ids[0, :, 0]
    onehot = (chosen[:, None] == jnp.arange(experts_in, dtype=jnp.int32)[None, :]).astype(jnp.int32)
    before = jnp.cumsum(onehot, axis=0, dtype=jnp.int32) - onehot
    slot_index = jnp.sum(before * onehot, axis=1, dtype=jnp.int32)
    target = chosen * CAP + slot_index
    source_row = jnp.full((experts_in * CAP,), tok_rows, jnp.int32).at[target].set(offsets)
    padded = jnp.concatenate([normed, jnp.zeros((1, width), jnp.bfloat16)], axis=0)
    outgoing = padded[source_row].reshape(group_devices, local_experts, CAP, width)
    incoming = lax.all_to_all(outgoing, "ep", split_axis=0, concat_axis=0, tiled=True)
    gate_part = jnp.einsum("secd,edf->secf", incoming, w_gate, preferred_element_type=jnp.float32)
    up_part = jnp.einsum("secd,edf->secf", incoming, w_up, preferred_element_type=jnp.float32)
    hidden = (jax.nn.silu(gate_part) * up_part).astype(jnp.bfloat16)
    returned = lax.all_to_all(
        jnp.einsum("secf,efd->secd", hidden, w_down, preferred_element_type=jnp.float32).astype(
            jnp.bfloat16
        ),
        "ep",
        split_axis=0,
        concat_axis=0,
        tiled=True,
    )
    expert_out = returned.reshape(experts_in * CAP, width)[target]
    layer_out = residual_wide + gate_prob[0] * expert_out.astype(jnp.float32)
    return layer_out.astype(jnp.bfloat16).reshape(1, tok_rows, width)


def solution(mesh):
    placed = (
        P("ep", "ctx", None),
        P("ep", "ctx", None),
        P("ep", "ctx", None),
        P("ep", "ctx", None),
        P("ep", None),
        P("ctx", None),
        P(),
        P("ep", "ctx", None),
        P("ep", "ctx", None),
        P("ep", None, None),
        P("ep", None, None),
        P("ep", None, None),
    )
    return jax.shard_map(
        on_device, mesh=mesh, in_specs=placed, out_specs=P("ep", "ctx", None), check_vma=False
    )
```

profile of v0, /device:TPU:128, one launch (start us, length us, event | category | flops | bytes accessed | tf_op | source)
XLA Modules:
  0.0 705.2 jit_solution(17172201404901420627)
XLA Ops:
  16.2 11.3 %conditional.2 = (f32[2,8,256]{2,1,0:T(8,128)}, f32[2,8,256]{2,1,0:T(8,128)S(1)}, f32[2,8,256,128]{3,2,1,0:T(8,128)}) conditional(s32[]{:T(128)} %convert_element_type.82, () %tuple.34, (pred[256,256]{0,1:T(8,128)(4,1)S(1)}, bf16[1,256,256]{2,1,0:T(8,128)(2,1)}, bf16[256,2,8,128]{0,3,2,1:T(8,128)(2,1)}, bf16[1,256,256]{2,1,0:T(8,128)(2,1)S(1)}) %tuple.80), branch_computations={%region_3.4_spmd, %region_4.0_spmd} | conditional | flops 548945920 | bytes 33669172 | solution.py:87
  27.5 557.1 %while.22 = (s32[]{:T(128)}, bf16[256,256]{1,0:T(8,128)(2,1)}, bf16[256,256]{1,0:T(8,128)(2,1)S(1)}, f32[2,8,256]{2,1,0:T(8,128)}, f32[2,8,256]{2,1,0:T(8,128)S(...) while((s32[]{:T(128)}, bf16[256,256]{1,0:T(8,128)(2,1)}, ...), condition=%wide.region_14.15_spmd.clone, body=%wide.region_7.14_spmd.clone.sunk | while | flops 549802752 | bytes 38020064 | solution.py:105
  46.1 12.1 %conditional.5 = ((f32[2,8,256]{2,1,0:T(8,128)}, f32[2,8,256]{2,1,0:T(8,128)S(1)}, f32[2,8,256,128]{3,2,1,0:T(8,128)})) conditional(s32[]{:T(128)} %convert_element_type.146, (f32[2,8,256]{2,1,0:T(8,128)}, f32[2,8,256]{2,1,0:T(8,128)S(1)}, f32[2,8,256,128]{3,2,1,0:T(8,128)}) %tuple.67, (pred[256,256]{0,1:T(8,128)(4,1)S(1)}, ...), branch_computations={%region_10.10_spmd, %region_11.13_spmd} | conditional | flops 549462016 | bytes 35848252 | solution.py:87
  51.8 5.8 multiply_add_fusion
  65.7 9.2 %collective-permute-done = bf16[256,256]{1,0:T(8,128)(2,1)S(1)} collective-permute-done((bf16[256,256]{1,0:T(8,128)(2,1)}, bf16[256,256]{1,0:T(8,128)(2,1)S(1)}, u32[]{:S(2)}, u32[]{:S(2)}) %collective-permute-start) | collective-permute-done | bytes 131104 | tf_op jit(solution)/shard_map/while/body/eval_jaxpr/ppermute | solution.py:19
  80.2 12.3 %conditional.5 = ((f32[2,8,256]{2,1,0:T(8,128)}, f32[2,8,256]{2,1,0:T(8,128)S(1)}, f32[2,8,256,128]{3,2,1,0:T(8,128)})) conditional(s32[]{:T(128)} %convert_element_type.146, (f32[2,8,256]{2,1,0:T(8,128)}, f32[2,8,256]{2,1,0:T(8,128)S(1)}, f32[2,8,256,128]{3,2,1,0:T(8,128)}) %tuple.67, (pred[256,256]{0,1:T(8,128)(4,1)S(1)}, ...), branch_computations={%region_10.10_spmd, %region_11.13_spmd} | conditional | flops 549462016 | bytes 35848252 | solution.py:87
  85.9 5.9 multiply_add_fusion
  100.0 9.2 %collective-permute-done = bf16[256,256]{1,0:T(8,128)(2,1)S(1)} collective-permute-done((bf16[256,256]{1,0:T(8,128)(2,1)}, bf16[256,256]{1,0:T(8,128)(2,1)S(1)}, u32[]{:S(2)}, u32[]{:S(2)}) %collective-permute-start) | collective-permute-done | bytes 131104 | tf_op jit(solution)/shard_map/while/body/eval_jaxpr/ppermute | solution.py:19
  116.3 9.6 %collective-permute-start = (bf16[256,256]{1,0:T(8,128)(2,1)}, bf16[256,256]{1,0:T(8,128)(2,1)S(1)}, u32[]{:S(2)}, u32[]{:S(2)}) collective-permute-start(bf16[256,256]{1,0:T(8,128)(2,1)} %get-tuple-element.474), channel_id=1, source_target_pairs={{0,8},{8,16},{16,24},{24,32},{32,40},{40,48},{48,56},{56,64},{64,7... | collective-permute-start | bytes 393224 | tf_op jit(solution)/shard_map/while/body/eval_jaxpr/ppermute | solution.py:19
  129.4 8.4 %collective-permute-done.1 = bf16[256,256]{1,0:T(8,128)(2,1)} collective-permute-done((bf16[256,256]{1,0:T(8,128)(2,1)}, bf16[256,256]{1,0:T(8,128)(2,1)}, u32[]{:S(2)}, u32[]{:S(2)}) %collective-permute-start.1) | collective-permute-done | bytes 131104 | tf_op jit(solution)/shard_map/while/body/eval_jaxpr/ppermute | solution.py:19
  141.9 9.3 %collective-permute-start.1 = (bf16[256,256]{1,0:T(8,128)(2,1)}, bf16[256,256]{1,0:T(8,128)(2,1)}, u32[]{:S(2)}, u32[]{:S(2)}) collective-permute-start(bf16[256,256]{1,0:T(8,128)(2,1)} %copy-done.5), channel_id=1, source_target_pairs={{0,8},{8,16},{16,24},{24,32},{32,40},{40,48},{48,56},{56,64},{64,7... | collective-permute-start | bytes 393224 | tf_op jit(solution)/shard_map/while/body/eval_jaxpr/ppermute | solution.py:19
  173.3 12.7 %collective-permute-start = (bf16[256,256]{1,0:T(8,128)(2,1)}, bf16[256,256]{1,0:T(8,128)(2,1)S(1)}, u32[]{:S(2)}, u32[]{:S(2)}) collective-permute-start(bf16[256,256]{1,0:T(8,128)(2,1)} %get-tuple-element.474), channel_id=1, source_target_pairs={{0,8},{8,16},{16,24},{24,32},{32,40},{40,48},{48,56},{56,64},{64,7... | collective-permute-start | bytes 393224 | tf_op jit(solution)/shard_map/while/body/eval_jaxpr/ppermute | solution.py:19
  200.6 14.9 %collective-permute-start.1 = (bf16[256,256]{1,0:T(8,128)(2,1)}, bf16[256,256]{1,0:T(8,128)(2,1)}, u32[]{:S(2)}, u32[]{:S(2)}) collective-permute-start(bf16[256,256]{1,0:T(8,128)(2,1)} %copy-done.5), channel_id=1, source_target_pairs={{0,8},{8,16},{16,24},{24,32},{32,40},{40,48},{48,56},{56,64},{64,7... | collective-permute-start | bytes 393224 | tf_op jit(solution)/shard_map/while/body/eval_jaxpr/ppermute | solution.py:19
  238.4 7.4 %collective-permute-start = (bf16[256,256]{1,0:T(8,128)(2,1)}, bf16[256,256]{1,0:T(8,128)(2,1)S(1)}, u32[]{:S(2)}, u32[]{:S(2)}) collective-permute-start(bf16[256,256]{1,0:T(8,128)(2,1)} %get-tuple-element.474), channel_id=1, source_target_pairs={{0,8},{8,16},{16,24},{24,32},{32,40},{40,48},{48,56},{56,64},{64,7... | collective-permute-start | bytes 393224 | tf_op jit(solution)/shard_map/while/body/eval_jaxpr/ppermute | solution.py:19
  245.9 6.5 collective-permute-start.1
  261.7 9.5 %collective-permute-start.1 = (bf16[256,256]{1,0:T(8,128)(2,1)}, bf16[256,256]{1,0:T(8,128)(2,1)}, u32[]{:S(2)}, u32[]{:S(2)}) collective-permute-start(bf16[256,256]{1,0:T(8,128)(2,1)} %copy-done.5), channel_id=1, source_target_pairs={{0,8},{8,16},{16,24},{24,32},{32,40},{40,48},{48,56},{56,64},{64,7... | collective-permute-start | bytes 393224 | tf_op jit(solution)/shard_map/while/body/eval_jaxpr/ppermute | solution.py:19
  281.7 7.5 %collective-permute-start.1 = (bf16[256,256]{1,0:T(8,128)(2,1)}, bf16[256,256]{1,0:T(8,128)(2,1)}, u32[]{:S(2)}, u32[]{:S(2)}) collective-permute-start(bf16[256,256]{1,0:T(8,128)(2,1)} %copy-done.5), channel_id=1, source_target_pairs={{0,8},{8,16},{16,24},{24,32},{32,40},{40,48},{48,56},{56,64},{64,7... | collective-permute-start | bytes 393224 | tf_op jit(solution)/shard_map/while/body/eval_jaxpr/ppermute | solution.py:19
  318.0 5.6 collective-permute-done
  333.1 6.3 collective-permute-done
  348.6 6.2 collective-permute-done
  363.9 5.8 collective-permute-done
  378.7 5.4 collective-permute-done
  512.0 6.4 collective-permute-done
  528.9 6.4 collective-permute-done
  544.8 6.3 collective-permute-done
  560.3 6.3 collective-permute-done
  575.7 5.9 collective-permute-done
  593.0 6.4 fusion.51
  601.8 6.7 gather_fusion
  608.5 37.7 %all_to_all.10 = bf16[8,1,64,2048]{3,2,1,0:T(8,128)(2,1)S(1)} all-to-all(bf16[8,1,64,2048]{3,2,1,0:T(8,128)(2,1)} %bitcast.145), channel_id=1, replica_groups=mesh['ctx'=32,'ep'=8] {'ep'}, dimensions={0} | all-to-all | bytes 4194304 | tf_op jit(solution)/shard_map/all_to_all | solution.py:135
  650.4 8.3 %fusion.47 = bf16[8,1,64,2048]{3,2,1,0:T(8,128)(2,1)} fusion(bf16[1,768,2048]{2,1,0:T(8,128)(2,1)S(1)} %copy-done, bf16[1,2048,768]{2,1,0:T(8,128)(2,1)} %param.28, bf16[8,1,64,2048]{3,2,1,0:T(8,128)(2,1)} %copy-done.4, f32[8,64,768]{2,1,0:T(8,128)} %fusion.42), kind=kOutput, calls=%fused_computation.57 | convolution fusion | flops 3224633344 | bytes 12058624 | tf_op jit(solution)/shard_map/secf,efd->secd/dot_general | solution.py:140
  663.3 27.0 %all-to-all-done.1 = bf16[8,1,64,2048]{3,2,1,0:T(8,128)(2,1)} async-done(((bf16[8,1,64,2048]{3,2,1,0:T(8,128)(2,1)}), bf16[8,1,64,2048]{3,2,1,0:T(8,128)(2,1)}, u32[]{:S(2)}, u32[]{:S(2)}) %all-to-all-start.1) | async-done | bytes 2097184 | tf_op jit(solution)/shard_map/all_to_all | solution.py:139
  (487 shorter events, 409.1 us)
Async XLA Ops:
  6.5 586.4 %all-gather.2.cloned.1.call-start = ((), (), s32[]{:S(2)}) async-start(), calls=%async_computation.2 | async-start | bytes 8650752 | tf_op jit(solution)/shard_map/all_gather | solution.py:115
  28.2 13.0 %collective-permute-start = (bf16[256,256]{1,0:T(8,128)(2,1)}, bf16[256,256]{1,0:T(8,128)(2,1)S(1)}, u32[]{:S(2)}, u32[]{:S(2)}) collective-permute-start(bf16[256,256]{1,0:T(8,128)(2,1)} %get-tuple-element.474), channel_id=1, source_target_pairs={{0,8},{8,16},{16,24},{24,32},{32,40},{40,48},{48,56},{56,64},{64,7... | collective-permute-start | bytes 393224 | tf_op jit(solution)/shard_map/while/body/eval_jaxpr/ppermute | solution.py:19
  31.7 14.4 %collective-permute-start.1 = (bf16[256,256]{1,0:T(8,128)(2,1)}, bf16[256,256]{1,0:T(8,128)(2,1)}, u32[]{:S(2)}, u32[]{:S(2)}) collective-permute-start(bf16[256,256]{1,0:T(8,128)(2,1)} %copy-done.5), channel_id=1, source_target_pairs={{0,8},{8,16},{16,24},{24,32},{32,40},{40,48},{48,56},{56,64},{64,7... | collective-permute-start | bytes 393224 | tf_op jit(solution)/shard_map/while/body/eval_jaxpr/ppermute | solution.py:19
  60.4 14.6 %collective-permute-start = (bf16[256,256]{1,0:T(8,128)(2,1)}, bf16[256,256]{1,0:T(8,128)(2,1)S(1)}, u32[]{:S(2)}, u32[]{:S(2)}) collective-permute-start(bf16[256,256]{1,0:T(8,128)(2,1)} %get-tuple-element.474), channel_id=1, source_target_pairs={{0,8},{8,16},{16,24},{24,32},{32,40},{40,48},{48,56},{56,64},{64,7... | collective-permute-start | bytes 393224 | tf_op jit(solution)/shard_map/while/body/eval_jaxpr/ppermute | solution.py:19
  62.3 17.9 %collective-permute-start.1 = (bf16[256,256]{1,0:T(8,128)(2,1)}, bf16[256,256]{1,0:T(8,128)(2,1)}, u32[]{:S(2)}, u32[]{:S(2)}) collective-permute-start(bf16[256,256]{1,0:T(8,128)(2,1)} %copy-done.5), channel_id=1, source_target_pairs={{0,8},{8,16},{16,24},{24,32},{32,40},{40,48},{48,56},{56,64},{64,7... | collective-permute-start | bytes 393224 | tf_op jit(solution)/shard_map/while/body/eval_jaxpr/ppermute | solution.py:19
  94.6 14.5 %collective-permute-start = (bf16[256,256]{1,0:T(8,128)(2,1)}, bf16[256,256]{1,0:T(8,128)(2,1)S(1)}, u32[]{:S(2)}, u32[]{:S(2)}) collective-permute-start(bf16[256,256]{1,0:T(8,128)(2,1)} %get-tuple-element.474), channel_id=1, source_target_pairs={{0,8},{8,16},{16,24},{24,32},{32,40},{40,48},{48,56},{56,64},{64,7... | collective-permute-start | bytes 393224 | tf_op jit(solution)/shard_map/while/body/eval_jaxpr/ppermute | solution.py:19
  96.6 17.6 %collective-permute-start.1 = (bf16[256,256]{1,0:T(8,128)(2,1)}, bf16[256,256]{1,0:T(8,128)(2,1)}, u32[]{:S(2)}, u32[]{:S(2)}) collective-permute-start(bf16[256,256]{1,0:T(8,128)(2,1)} %copy-done.5), channel_id=1, source_target_pairs={{0,8},{8,16},{16,24},{24,32},{32,40},{40,48},{48,56},{56,64},{64,7... | collective-permute-start | bytes 393224 | tf_op jit(solution)/shard_map/while/body/eval_jaxpr/ppermute | solution.py:19
  116.3 13.0 %collective-permute-start = (bf16[256,256]{1,0:T(8,128)(2,1)}, bf16[256,256]{1,0:T(8,128)(2,1)S(1)}, u32[]{:S(2)}, u32[]{:S(2)}) collective-permute-start(bf16[256,256]{1,0:T(8,128)(2,1)} %get-tuple-element.474), channel_id=1, source_target_pairs={{0,8},{8,16},{16,24},{24,32},{32,40},{40,48},{48,56},{56,64},{64,7... | collective-permute-start | bytes 393224 | tf_op jit(solution)/shard_map/while/body/eval_jaxpr/ppermute | solution.py:19
  125.9 11.8 %collective-permute-start.1 = (bf16[256,256]{1,0:T(8,128)(2,1)}, bf16[256,256]{1,0:T(8,128)(2,1)}, u32[]{:S(2)}, u32[]{:S(2)}) collective-permute-start(bf16[256,256]{1,0:T(8,128)(2,1)} %copy-done.5), channel_id=1, source_target_pairs={{0,8},{8,16},{16,24},{24,32},{32,40},{40,48},{48,56},{56,64},{64,7... | collective-permute-start | bytes 393224 | tf_op jit(solution)/shard_map/while/body/eval_jaxpr/ppermute | solution.py:19
  140.0 12.8 %collective-permute-start = (bf16[256,256]{1,0:T(8,128)(2,1)}, bf16[256,256]{1,0:T(8,128)(2,1)S(1)}, u32[]{:S(2)}, u32[]{:S(2)}) collective-permute-start(bf16[256,256]{1,0:T(8,128)(2,1)} %get-tuple-element.474), channel_id=1, source_target_pairs={{0,8},{8,16},{16,24},{24,32},{32,40},{40,48},{48,56},{56,64},{64,7... | collective-permute-start | bytes 393224 | tf_op jit(solution)/shard_map/while/body/eval_jaxpr/ppermute | solution.py:19
  141.9 12.2 %collective-permute-start.1 = (bf16[256,256]{1,0:T(8,128)(2,1)}, bf16[256,256]{1,0:T(8,128)(2,1)}, u32[]{:S(2)}, u32[]{:S(2)}) collective-permute-start(bf16[256,256]{1,0:T(8,128)(2,1)} %copy-done.5), channel_id=1, source_target_pairs={{0,8},{8,16},{16,24},{24,32},{32,40},{40,48},{48,56},{56,64},{64,7... | collective-permute-start | bytes 393224 | tf_op jit(solution)/shard_map/while/body/eval_jaxpr/ppermute | solution.py:19
  173.3 18.5 %collective-permute-start = (bf16[256,256]{1,0:T(8,128)(2,1)}, bf16[256,256]{1,0:T(8,128)(2,1)S(1)}, u32[]{:S(2)}, u32[]{:S(2)}) collective-permute-start(bf16[256,256]{1,0:T(8,128)(2,1)} %get-tuple-element.474), channel_id=1, source_target_pairs={{0,8},{8,16},{16,24},{24,32},{32,40},{40,48},{48,56},{56,64},{64,7... | collective-permute-start | bytes 393224 | tf_op jit(solution)/shard_map/while/body/eval_jaxpr/ppermute | solution.py:19
  198.7 18.3 %collective-permute-start = (bf16[256,256]{1,0:T(8,128)(2,1)}, bf16[256,256]{1,0:T(8,128)(2,1)S(1)}, u32[]{:S(2)}, u32[]{:S(2)}) collective-permute-start(bf16[256,256]{1,0:T(8,128)(2,1)} %get-tuple-element.474), channel_id=1, source_target_pairs={{0,8},{8,16},{16,24},{24,32},{32,40},{40,48},{48,56},{56,64},{64,7... | collective-permute-start | bytes 393224 | tf_op jit(solution)/shard_map/while/body/eval_jaxpr/ppermute | solution.py:19
  200.6 17.7 %collective-permute-start.1 = (bf16[256,256]{1,0:T(8,128)(2,1)}, bf16[256,256]{1,0:T(8,128)(2,1)}, u32[]{:S(2)}, u32[]{:S(2)}) collective-permute-start(bf16[256,256]{1,0:T(8,128)(2,1)} %copy-done.5), channel_id=1, source_target_pairs={{0,8},{8,16},{16,24},{24,32},{32,40},{40,48},{48,56},{56,64},{64,7... | collective-permute-start | bytes 393224 | tf_op jit(solution)/shard_map/while/body/eval_jaxpr/ppermute | solution.py:19
  238.4 15.4 %collective-permute-start = (bf16[256,256]{1,0:T(8,128)(2,1)}, bf16[256,256]{1,0:T(8,128)(2,1)S(1)}, u32[]{:S(2)}, u32[]{:S(2)}) collective-permute-start(bf16[256,256]{1,0:T(8,128)(2,1)} %get-tuple-element.474), channel_id=1, source_target_pairs={{0,8},{8,16},{16,24},{24,32},{32,40},{40,48},{48,56},{56,64},{64,7... | collective-permute-start | bytes 393224 | tf_op jit(solution)/shard_map/while/body/eval_jaxpr/ppermute | solution.py:19
  258.6 14.1 %collective-permute-start = (bf16[256,256]{1,0:T(8,128)(2,1)}, bf16[256,256]{1,0:T(8,128)(2,1)S(1)}, u32[]{:S(2)}, u32[]{:S(2)}) collective-permute-start(bf16[256,256]{1,0:T(8,128)(2,1)} %get-tuple-element.474), channel_id=1, source_target_pairs={{0,8},{8,16},{16,24},{24,32},{32,40},{40,48},{48,56},{56,64},{64,7... | collective-permute-start | bytes 393224 | tf_op jit(solution)/shard_map/while/body/eval_jaxpr/ppermute | solution.py:19
  261.7 13.4 %collective-permute-start.1 = (bf16[256,256]{1,0:T(8,128)(2,1)}, bf16[256,256]{1,0:T(8,128)(2,1)}, u32[]{:S(2)}, u32[]{:S(2)}) collective-permute-start(bf16[256,256]{1,0:T(8,128)(2,1)} %copy-done.5), channel_id=1, source_target_pairs={{0,8},{8,16},{16,24},{24,32},{32,40},{40,48},{48,56},{56,64},{64,7... | collective-permute-start | bytes 393224 | tf_op jit(solution)/shard_map/while/body/eval_jaxpr/ppermute | solution.py:19
  277.3 13.3 %collective-permute-start = (bf16[256,256]{1,0:T(8,128)(2,1)}, bf16[256,256]{1,0:T(8,128)(2,1)S(1)}, u32[]{:S(2)}, u32[]{:S(2)}) collective-permute-start(bf16[256,256]{1,0:T(8,128)(2,1)} %get-tuple-element.474), channel_id=1, source_target_pairs={{0,8},{8,16},{16,24},{24,32},{32,40},{40,48},{48,56},{56,64},{64,7... | collective-permute-start | bytes 393224 | tf_op jit(solution)/shard_map/while/body/eval_jaxpr/ppermute | solution.py:19
  281.7 11.9 %collective-permute-start.1 = (bf16[256,256]{1,0:T(8,128)(2,1)}, bf16[256,256]{1,0:T(8,128)(2,1)}, u32[]{:S(2)}, u32[]{:S(2)}) collective-permute-start(bf16[256,256]{1,0:T(8,128)(2,1)} %copy-done.5), channel_id=1, source_target_pairs={{0,8},{8,16},{16,24},{24,32},{32,40},{40,48},{48,56},{56,64},{64,7... | collective-permute-start | bytes 393224 | tf_op jit(solution)/shard_map/while/body/eval_jaxpr/ppermute | solution.py:19
  295.8 11.7 %collective-permute-start = (bf16[256,256]{1,0:T(8,128)(2,1)}, bf16[256,256]{1,0:T(8,128)(2,1)S(1)}, u32[]{:S(2)}, u32[]{:S(2)}) collective-permute-start(bf16[256,256]{1,0:T(8,128)(2,1)} %get-tuple-element.474), channel_id=1, source_target_pairs={{0,8},{8,16},{16,24},{24,32},{32,40},{40,48},{48,56},{56,64},{64,7... | collective-permute-start | bytes 393224 | tf_op jit(solution)/shard_map/while/body/eval_jaxpr/ppermute | solution.py:19
  298.6 11.4 %collective-permute-start.1 = (bf16[256,256]{1,0:T(8,128)(2,1)}, bf16[256,256]{1,0:T(8,128)(2,1)}, u32[]{:S(2)}, u32[]{:S(2)}) collective-permute-start(bf16[256,256]{1,0:T(8,128)(2,1)} %copy-done.5), channel_id=1, source_target_pairs={{0,8},{8,16},{16,24},{24,32},{32,40},{40,48},{48,56},{56,64},{64,7... | collective-permute-start | bytes 393224 | tf_op jit(solution)/shard_map/while/body/eval_jaxpr/ppermute | solution.py:19
  314.1 11.4 %collective-permute-start.1 = (bf16[256,256]{1,0:T(8,128)(2,1)}, bf16[256,256]{1,0:T(8,128)(2,1)}, u32[]{:S(2)}, u32[]{:S(2)}) collective-permute-start(bf16[256,256]{1,0:T(8,128)(2,1)} %copy-done.5), channel_id=1, source_target_pairs={{0,8},{8,16},{16,24},{24,32},{32,40},{40,48},{48,56},{56,64},{64,7... | collective-permute-start | bytes 393224 | tf_op jit(solution)/shard_map/while/body/eval_jaxpr/ppermute | solution.py:19
  327.7 11.7 %collective-permute-start = (bf16[256,256]{1,0:T(8,128)(2,1)}, bf16[256,256]{1,0:T(8,128)(2,1)S(1)}, u32[]{:S(2)}, u32[]{:S(2)}) collective-permute-start(bf16[256,256]{1,0:T(8,128)(2,1)} %get-tuple-element.474), channel_id=1, source_target_pairs={{0,8},{8,16},{16,24},{24,32},{32,40},{40,48},{48,56},{56,64},{64,7... | collective-permute-start | bytes 393224 | tf_op jit(solution)/shard_map/while/body/eval_jaxpr/ppermute | solution.py:19
  343.2 11.6 %collective-permute-start = (bf16[256,256]{1,0:T(8,128)(2,1)}, bf16[256,256]{1,0:T(8,128)(2,1)S(1)}, u32[]{:S(2)}, u32[]{:S(2)}) collective-permute-start(bf16[256,256]{1,0:T(8,128)(2,1)} %get-tuple-element.474), channel_id=1, source_target_pairs={{0,8},{8,16},{16,24},{24,32},{32,40},{40,48},{48,56},{56,64},{64,7... | collective-permute-start | bytes 393224 | tf_op jit(solution)/shard_map/while/body/eval_jaxpr/ppermute | solution.py:19
  492.6 11.9 %collective-permute-start.1 = (bf16[256,256]{1,0:T(8,128)(2,1)}, bf16[256,256]{1,0:T(8,128)(2,1)}, u32[]{:S(2)}, u32[]{:S(2)}) collective-permute-start(bf16[256,256]{1,0:T(8,128)(2,1)} %copy-done.5), channel_id=1, source_target_pairs={{0,8},{8,16},{16,24},{24,32},{32,40},{40,48},{48,56},{56,64},{64,7... | collective-permute-start | bytes 393224 | tf_op jit(solution)/shard_map/while/body/eval_jaxpr/ppermute | solution.py:19
  506.7 11.8 %collective-permute-start = (bf16[256,256]{1,0:T(8,128)(2,1)}, bf16[256,256]{1,0:T(8,128)(2,1)S(1)}, u32[]{:S(2)}, u32[]{:S(2)}) collective-permute-start(bf16[256,256]{1,0:T(8,128)(2,1)} %get-tuple-element.474), channel_id=1, source_target_pairs={{0,8},{8,16},{16,24},{24,32},{32,40},{40,48},{48,56},{56,64},{64,7... | collective-permute-start | bytes 393224 | tf_op jit(solution)/shard_map/while/body/eval_jaxpr/ppermute | solution.py:19
  508.6 12.7 %collective-permute-start.1 = (bf16[256,256]{1,0:T(8,128)(2,1)}, bf16[256,256]{1,0:T(8,128)(2,1)}, u32[]{:S(2)}, u32[]{:S(2)}) collective-permute-start(bf16[256,256]{1,0:T(8,128)(2,1)} %copy-done.5), channel_id=1, source_target_pairs={{0,8},{8,16},{16,24},{24,32},{32,40},{40,48},{48,56},{56,64},{64,7... | collective-permute-start | bytes 393224 | tf_op jit(solution)/shard_map/while/body/eval_jaxpr/ppermute | solution.py:19
  523.5 11.7 %collective-permute-start = (bf16[256,256]{1,0:T(8,128)(2,1)}, bf16[256,256]{1,0:T(8,128)(2,1)S(1)}, u32[]{:S(2)}, u32[]{:S(2)}) collective-permute-start(bf16[256,256]{1,0:T(8,128)(2,1)} %get-tuple-element.474), channel_id=1, source_target_pairs={{0,8},{8,16},{16,24},{24,32},{32,40},{40,48},{48,56},{56,64},{64,7... | collective-permute-start | bytes 393224 | tf_op jit(solution)/shard_map/while/body/eval_jaxpr/ppermute | solution.py:19
  525.4 11.9 %collective-permute-start.1 = (bf16[256,256]{1,0:T(8,128)(2,1)}, bf16[256,256]{1,0:T(8,128)(2,1)}, u32[]{:S(2)}, u32[]{:S(2)}) collective-permute-start(bf16[256,256]{1,0:T(8,128)(2,1)} %copy-done.5), channel_id=1, source_target_pairs={{0,8},{8,16},{16,24},{24,32},{32,40},{40,48},{48,56},{56,64},{64,7... | collective-permute-start | bytes 393224 | tf_op jit(solution)/shard_map/while/body/eval_jaxpr/ppermute | solution.py:19
  539.5 11.6 %collective-permute-start = (bf16[256,256]{1,0:T(8,128)(2,1)}, bf16[256,256]{1,0:T(8,128)(2,1)S(1)}, u32[]{:S(2)}, u32[]{:S(2)}) collective-permute-start(bf16[256,256]{1,0:T(8,128)(2,1)} %get-tuple-element.474), channel_id=1, source_target_pairs={{0,8},{8,16},{16,24},{24,32},{32,40},{40,48},{48,56},{56,64},{64,7... | collective-permute-start | bytes 393224 | tf_op jit(solution)/shard_map/while/body/eval_jaxpr/ppermute | solution.py:19
  555.0 11.6 %collective-permute-start = (bf16[256,256]{1,0:T(8,128)(2,1)}, bf16[256,256]{1,0:T(8,128)(2,1)S(1)}, u32[]{:S(2)}, u32[]{:S(2)}) collective-permute-start(bf16[256,256]{1,0:T(8,128)(2,1)} %get-tuple-element.474), channel_id=1, source_target_pairs={{0,8},{8,16},{16,24},{24,32},{32,40},{40,48},{48,56},{56,64},{64,7... | collective-permute-start | bytes 393224 | tf_op jit(solution)/shard_map/while/body/eval_jaxpr/ppermute | solution.py:19
  658.7 31.6 %all-to-all-start.1 = ((bf16[8,1,64,2048]{3,2,1,0:T(8,128)(2,1)}), bf16[8,1,64,2048]{3,2,1,0:T(8,128)(2,1)}, u32[]{:S(2)}, u32[]{:S(2)}) async-start(bf16[8,1,64,2048]{3,2,1,0:T(8,128)(2,1)} %fusion.47), calls=%async_computation.1 | async-start | bytes 4194304 | tf_op jit(solution)/shard_map/all_to_all | solution.py:139
  (73 other events, 1069.2 us)
Sparse Core Ops, SparseCore 0:
  9.9 109.3 all-gather.1
where the time goes:
time: 710 us; the launch traced here: 705 us
  waiting for transfers between devices  240 us (34%)
  starting transfers between devices  209 us (29%)
  local copies, waits for them, and re-layouts  101 us (14%)
  other arithmetic  42.9 us (6%)
  matrix products  40.8 us (6%)
  blocking collectives  37.7 us (5%)
  loops' own time  19.4 us (3%)
  between operations  14.2 us (2%)
    ppermute x62, waiting for transfers between devices, from_behind(): return lax.ppermute(array, axis, pairs)  213 us
    ppermute x62, starting transfers between devices, from_behind(): return lax.ppermute(array, axis, pairs)  204 us
    while x124, local copies, waits for them, and re-layouts  68.3 us
    all_to_all x1, blocking collectives, on_device(): lax.all_to_all(outgoing, 'ep', split_axis=0, concat_axis=0, tiled=True)  37.7 us
    all_to_all x1, waiting for transfers between devices, on_device(): lax.all_to_all(jnp.einsum('secf,efd->secd', hidden, w_down, preferred_ele...  27 us
    reduce_or x31, other arithmetic, absorb(): return lax.cond(jnp.any(visible), update, lambda carry: carry, state)  24.2 us
    another operation x1, loops' own time, on_device(): final = lax.fori_loop(1, cycle_size, circle, (keys[0], values[0], state))  19.3 us
    dot_general x3, matrix products, update(): jnp.einsum('hgqk,khd->hgqd', weights.astype(jnp.bfloat16), value_tile_blo...  17 us
  transfers between devices with their start and end apart: 64, of which 55 were waited for; matrix products, arithmetic and copies ran while one was open for 18% of the time, Pallas kernels for 0%

commit v1 on v0

v1 whole, which is shorter than its diff:
```python
import math

import jax
import jax.numpy as jnp
from jax import lax
from jax.experimental import pallas as pl
from jax.experimental.pallas import tpu as pltpu
from jax.sharding import PartitionSpec as P

HEAD = 128
CAP = 64
GROUP = 8

masked_value = -1e30
norm_epsilon = 1e-06
BF = jnp.bfloat16
F32 = jnp.float32


def call(body, out_shape, name, vmem_mb=48, **kw):
    return pl.pallas_call(
        body,
        out_shape=out_shape,
        name=name,
        compiler_params=pltpu.CompilerParams(vmem_limit_bytes=vmem_mb * 1024 * 1024),
        **kw,
    )


def dot(a, b, dims=((1,), (0,))):
    return lax.dot_general(a, b, (dims, ((), ())), preferred_element_type=F32)


def attention_body(info, start, q, own, recv, out, acc, run_max, run_sum):
    rows = q.shape[0]
    heads = q.shape[1] // HEAD
    kv_heads = own.shape[1] // (2 * HEAD)
    per = heads // kv_heads
    factor = math.log2(math.e) / math.sqrt(HEAD)
    block, pos_in_group, n_full, n_active = info[0], info[1], info[2], info[3]
    key_iota = lax.broadcasted_iota(jnp.int32, (rows, rows), 0)
    query_iota = lax.broadcasted_iota(jnp.int32, (rows, rows), 1)

    def step(load, key_start, first, masked):
        if masked:
            key_pos = key_iota + key_start
            seen = (key_pos >= start[...]) & (key_pos <= query_iota + block * rows)
        for g in range(kv_heads):
            k = load(slice(None), slice(g * HEAD, (g + 1) * HEAD))
            vt = load(slice(g * HEAD, (g + 1) * HEAD), slice(kv_heads * HEAD, kv_heads * HEAD + rows))
            for i in range(per):
                h = g * per + i
                s = dot(k, q[:, h * HEAD : (h + 1) * HEAD], ((1,), (1,)))
                if masked:
                    s = jnp.where(seen, s, masked_value)
                top = jnp.max(s, axis=0, keepdims=True)
                if not first:
                    old = run_max[h]
                    top = jnp.maximum(old, top)
                    scale = jnp.exp2((old - top) * factor)
                w = jnp.exp2((s - top) * factor)
                total = jnp.sum(w, axis=0, keepdims=True)
                mixed = dot(vt, w.astype(BF))
                if first:
                    run_sum[h] = total
                    acc[h] = mixed
                else:
                    run_sum[h] = run_sum[h] * scale + total
                    acc[h] = acc[h] * scale + mixed
                run_max[h] = top

    step(lambda a, b: own[a, b], block * rows, True, True)

    def other(d, masked):
        src = lax.rem(pos_in_group - d + 2 * GROUP, GROUP)
        step(lambda a, b: recv[src, a, b], (block - d) * rows, False, masked)

    def full(d, c):
        other(d, False)
        return c

    def part(d, c):
        other(d, True)
        return c

    lax.fori_loop(1, n_full, full, 0)
    lax.fori_loop(n_full, n_active, part, 0)
    for h in range(heads):
        out[:, h * HEAD : (h + 1) * HEAD] = (acc[h] / run_sum[h]).T.astype(BF)


def project_body(attn, w, tokens, gain, target, residual, outgoing, wide):
    t = pl.program_id(0)
    cols = w.shape[1]
    here = pl.ds(pl.multiple_of(t * cols, cols), cols)
    res = (tokens[:, here].astype(F32) + dot(attn[...], w[...])).astype(BF)
    residual[:, here] = res

    @pl.when(t == pl.num_programs(0) - 1)
    def _():
        x = residual[...].astype(F32)
        mean = jnp.mean(x * x, axis=-1, keepdims=True)
        wide[...] = (x * lax.rsqrt(mean + norm_epsilon) * gain[...]).astype(BF)
        slots = outgoing.shape[0]
        rows = residual.shape[0]
        pick = (lax.broadcasted_iota(jnp.int32, (slots, rows), 0) == target[...]).astype(BF)
        outgoing[...] = dot(pick, wide[...]).astype(BF)


def expert_body(x, w_gate, w_up, w_down, out, acc):
    t = pl.program_id(0)
    gate = dot(x[...], w_gate[...])
    up = dot(x[...], w_up[...])
    hidden = (gate / (1.0 + jnp.exp(-gate)) * up).astype(BF)
    part = dot(hidden, w_down[...])

    @pl.when(t == 0)
    def _():
        acc[...] = part

    @pl.when(t > 0)
    def _():
        acc[...] += part

    @pl.when(t == pl.num_programs(0) - 1)
    def _():
        out[...] = acc[...].astype(BF)


def combine_body(returned, residual, gate_prob, target, out):
    slots = returned.shape[0]
    rows = residual.shape[0]
    pick = (lax.broadcasted_iota(jnp.int32, (rows, slots), 1) == target[...]).astype(BF)
    back = dot(pick, returned[...])
    out[...] = (residual[...].astype(F32) + gate_prob[...] * back).astype(BF)


def on_device(
    tokens,
    queries,
    keys,
    values,
    lengths,
    out_proj,
    norm_gain,
    expert_ids,
    gate_prob,
    w_gate,
    w_up,
    w_down,
):
    rows = tokens.shape[1]
    width = tokens.shape[2]
    heads = queries.shape[2] // HEAD
    n_ctx = lax.axis_size("ctx")
    n_ep = lax.axis_size("ep")
    me = lax.axis_index("ctx")
    slot = lax.rem(me, GROUP)
    groups = [[g * GROUP + i for i in range(GROUP)] for g in range(n_ctx // GROUP)]

    pair = jnp.concatenate([keys[0], values[0].T], axis=1)
    behind = lax.ppermute(pair, "ctx", [(i, (i + GROUP) % n_ctx) for i in range(n_ctx)])
    ahead = jnp.arange(GROUP, dtype=jnp.int32)[:, None, None] > slot
    payload = jnp.where(ahead, pair[None], behind[None])
    recv = lax.all_to_all(payload, "ctx", 0, 0, axis_index_groups=groups)
    weight = lax.all_gather(out_proj, "ctx", axis=0, tiled=True)

    bounds = jnp.cumsum(lengths[0], dtype=jnp.int32)
    offsets = jnp.arange(rows, dtype=jnp.int32)
    pos = me * rows + offsets
    start = jnp.max(jnp.where(bounds[None, :] <= pos[:, None], bounds[None, :], 0), axis=1)
    n_active = me - start[0] // rows + 1
    n_full = me - (start[rows - 1] + rows - 1) // rows + 1
    n_full = jnp.clip(n_full, 1, n_active)
    info = jnp.stack([me, slot, n_full, n_active]).astype(jnp.int32)

    smem = pl.BlockSpec(memory_space=pltpu.SMEM)
    vmem = pl.BlockSpec(memory_space=pltpu.VMEM)
    attn = call(
        attention_body,
        jax.ShapeDtypeStruct((rows, width), BF),
        "attention",
        in_specs=[smem, vmem, vmem, vmem, vmem],
        out_specs=vmem,
        scratch_shapes=[
            pltpu.VMEM((heads, HEAD, rows), F32),
            pltpu.VMEM((heads, 1, rows), F32),
            pltpu.VMEM((heads, 1, rows), F32),
        ],
    )(info, start[None, :], queries[0], pair, recv)

    chosen = expert_ids[0, :, 0]
    n_experts = w_gate.shape[0] * n_ep
    slots = n_experts * CAP
    onehot = (chosen[:, None] == jnp.arange(n_experts, dtype=jnp.int32)[None, :]).astype(jnp.int32)
    before = jnp.cumsum(onehot, axis=0, dtype=jnp.int32) - onehot
    target = chosen * CAP + jnp.sum(before * onehot, axis=1, dtype=jnp.int32)

    tile = 256
    residual, outgoing = call(
        project_body,
        (jax.ShapeDtypeStruct((rows, width), BF), jax.ShapeDtypeStruct((slots, width), BF)),
        "project",
        grid=(width // tile,),
        in_specs=[
            pl.BlockSpec((rows, width), lambda t: (0, 0)),
            pl.BlockSpec((width, tile), lambda t: (0, t)),
            pl.BlockSpec((rows, width), lambda t: (0, 0)),
            pl.BlockSpec((1, width), lambda t: (0, 0)),
            pl.BlockSpec((1, rows), lambda t: (0, 0)),
        ],
        out_specs=(
            pl.BlockSpec((rows, width), lambda t: (0, 0)),
            pl.BlockSpec((slots, width), lambda t: (0, 0)),
        ),
        scratch_shapes=[pltpu.VMEM((rows, width), BF)],
    )(attn, weight, tokens[0], norm_gain[None, :], target[None, :])

    incoming = lax.all_to_all(outgoing.reshape(n_ep, slots // n_ep, width), "ep", 0, 0)
    incoming = incoming.reshape(slots, width)
    ffe = w_gate.shape[2]
    expert_out = call(
        expert_body,
        jax.ShapeDtypeStruct((slots, width), BF),
        "experts",
        grid=(ffe // tile,),
        in_specs=[
            pl.BlockSpec((slots, width), lambda t: (0, 0)),
            pl.BlockSpec((width, tile), lambda t: (0, t)),
            pl.BlockSpec((width, tile), lambda t: (0, t)),
            pl.BlockSpec((tile, width), lambda t: (t, 0)),
        ],
        out_specs=pl.BlockSpec((slots, width), lambda t: (0, 0)),
        scratch_shapes=[pltpu.VMEM((slots, width), F32)],
    )(incoming, w_gate[0], w_up[0], w_down[0])
    returned = lax.all_to_all(expert_out.reshape(n_ep, slots // n_ep, width), "ep", 0, 0)
    returned = returned.reshape(slots, width)

    layer_out = call(
        combine_body,
        jax.ShapeDtypeStruct((rows, width), BF),
        "combine",
        in_specs=[vmem, vmem, vmem, vmem],
        out_specs=vmem,
    )(returned, residual, gate_prob[0], target[:, None])
    return layer_out[None]


def solution(mesh):
    placed = (
        P("ep", "ctx", None),
        P("ep", "ctx", None),
        P("ep", "ctx", None),
        P("ep", "ctx", None),
        P("ep", None),
        P("ctx", None),
        P(),
        P("ep", "ctx", None),
        P("ep", "ctx", None),
        P("ep", None, None),
        P("ep", None, None),
        P("ep", None, None),
    )
    return jax.shard_map(
        on_device, mesh=mesh, in_specs=placed, out_specs=P("ep", "ctx", None), check_vma=False
    )
```

time: 710 us -> 205 us (0.29)
  the two profiles are of different devices: /device:TPU:128 before, /device:TPU:1 now
where the time goes in v1:
time: 205 us; the launch traced here: 204 us
  waiting for transfers between devices  103 us (50%)
  blocking collectives  31.6 us (15%)
  Pallas kernels  24.7 us (12%)
  starting transfers between devices  17.7 us (9%)
  between operations  16.4 us (8%)
  local copies, waits for them, and re-layouts  7 us (3%)
  other arithmetic  3.64 us (2%)
    all_gather x1, waiting for transfers between devices, on_device(): weight = lax.all_gather(out_proj, 'ctx', axis=0, tiled=True)  39.3 us
    all_to_all x1, blocking collectives, on_device(): lax.all_to_all(outgoing.reshape(n_ep, slots // n_ep, width), 'ep', 0, 0)  31.6 us
    all_to_all x1, waiting for transfers between devices, on_device(): recv = lax.all_to_all(payload, 'ctx', 0, 0, axis_index_groups=groups)  26.4 us
    all_to_all x1, waiting for transfers between devices, on_device(): lax.all_to_all(expert_out.reshape(n_ep, slots // n_ep, width), 'ep', 0, 0)  26.1 us
    ppermute x1, waiting for transfers between devices, on_device(): lax.ppermute(pair, 'ctx', [(i, (i + GROUP) % n_ctx) for i in range(n_ctx)])  10.6 us
    all_to_all x1, starting transfers between devices, on_device(): recv = lax.all_to_all(payload, 'ctx', 0, 0, axis_index_groups=groups)  9.14 us
    pallas_call x1, Pallas kernels, on_device(): call(expert_body, jax.ShapeDtypeStruct((slots, width), BF), 'experts', gr...  8.63 us
    pallas_call x1, Pallas kernels, on_device(): call(project_body, (jax.ShapeDtypeStruct((rows, width), BF), jax.ShapeDty...  8.45 us
  transfers between devices with their start and end apart: 4, of which 4 were waited for; matrix products, arithmetic and copies ran while one was open for 3% of the time, Pallas kernels for 3%

profile of v1, /device:TPU:1, one launch (start us, length us, event | category | flops | bytes accessed | tf_op | source)
XLA Modules:
  0.0 204.1 jit_solution(6993861932594506195)
XLA Ops:
  6.5 0.0 all-gather.2.cloned.1.call-start
  6.5 0.7 all-gather.2.cloned.1.call-update
  7.3 1.0 copy.26
  8.3 0.9 pad_maximum_fusion.own
  9.2 3.9 %collective-permute-start = (bf16[256,512]{1,0:T(8,128)(2,1)S(1)}, bf16[256,512]{1,0:T(8,128)(2,1)S(1)}, u32[]{:S(2)}, u32[]{:S(2)}) collective-permute-start(bf16[256,512]{1,0:T(8,128)(2,1)S(1)} %pad_maximum_fusion.own), channel_id=1, source_target_pairs={{0,64},{8,72},{16,80},{24,88},{32,96},{40,104},{48,112},{56,120},{... | collective-permute-start | bytes 786440 | tf_op jit(solution)/shard_map/ppermute | solution.py:162
  13.1 10.6 %collective-permute-done = bf16[256,512]{1,0:T(8,128)(2,1)S(1)} collective-permute-done((bf16[256,512]{1,0:T(8,128)(2,1)S(1)}, bf16[256,512]{1,0:T(8,128)(2,1)S(1)}, u32[]{:S(2)}, u32[]{:S(2)}) %collective-permute-start) | collective-permute-done | bytes 262176 | tf_op jit(solution)/shard_map/ppermute | solution.py:162
  23.7 1.7 broadcast_select_fusion
  25.4 9.1 %all-to-all-start = ((bf16[8,256,512]{2,1,0:T(8,128)(2,1)}), bf16[8,256,512]{2,1,0:T(8,128)(2,1)S(1)}, u32[]{:S(2)}, u32[]{:S(2)}) async-start(bf16[8,256,512]{2,1,0:T(8,128)(2,1)} %broadcast_select_fusion), calls=%async_computation | async-start | bytes 4194304 | tf_op jit(solution)/shard_map/all_to_all | solution.py:165
  34.5 0.1 copy.25
  34.6 0.1 reduce
  34.8 0.1 select_reduce_fusion
  34.9 0.6 fusion.3
  38.4 0.6 reduce-window.19
  39.0 0.2 slice_reduce_fusion
  39.3 0.1 pad_add_fusion.info
  39.4 0.1 fusion.1
  39.5 26.4 %all-to-all-done.recv = bf16[8,256,512]{2,1,0:T(8,128)(2,1)S(1)} async-done(((bf16[8,256,512]{2,1,0:T(8,128)(2,1)}), bf16[8,256,512]{2,1,0:T(8,128)(2,1)S(1)}, u32[]{:S(2)}, u32[]{:S(2)}) %all-to-all-start) | async-done | bytes 2097184 | tf_op jit(solution)/shard_map/all_to_all | solution.py:165
  65.8 1.2 copy-done.4
  67.1 5.8 %attention.1.attn = bf16[256,2048]{1,0:T(8,128)(2,1)S(1)} custom-call(s32[4]{0:T(128)S(1)} %pad_add_fusion.info, s32[1,256]{1,0:T(1,128)S(1)} %bitcast.46, bf16[256,2048]{1,0:T(8,128)(2,1)S(1)} %bitcast.45, bf16[256,512]{1,0:T(8,128)(2,1)S(1)} %pad_maximum_fusion.own, bf16[8,256,512]{2,1,0:T(8,128)(2,1)S(1)} %all-to-all-done.recv), custom_call_target="tpu_custom_call" | custom-call | tf_op jit(solution)/shard_map/attention/pallas_call | solution.py:179
  72.9 39.3 %all-gather.2.cloned.1.call-done.w = bf16[2048,2048]{1,0:T(8,128)(2,1)} async-done(((bf16[64,2048]{1,0:T(8,128)(2,1)}), bf16[2048,2048]{1,0:T(8,128)(2,1)}) %all-gather.2.cloned.1.call-update) | async-done | bytes 8388624 | tf_op jit(solution)/shard_map/all_gather | solution.py:166
  112.2 1.2 copy-done.1
  113.4 8.4 %project.1 = (bf16[256,2048]{1,0:T(8,128)(2,1)S(1)}, bf16[512,2048]{1,0:T(8,128)(2,1)S(1)}) custom-call(bf16[256,2048]{1,0:T(8,128)(2,1)S(1)} %attention.1.attn, bf16[2048,2048]{1,0:T(8,128)(2,1)} %all-gather.2.cloned.1.call-done.w, bf16[256,2048]{1,0:T(8,128)(2,1)S(1)} %bitcast.44, f32[1,2048]{1,0:T(1,128)S(1)} %bitcast.47, ...), custom_call_target="tpu_custom_call" | custom-call | tf_op jit(solution)/shard_map/project/pallas_call | solution.py:200
  121.9 0.0 copy-start.2
  121.9 1.0 copy-done.2
  122.9 31.6 %all_to_all.15 = bf16[8,64,2048]{2,1,0:T(8,128)(2,1)S(1)} all-to-all(bf16[8,64,2048]{2,1,0:T(8,128)(2,1)S(1)} %bitcast.43), channel_id=1, replica_groups=mesh['ctx'=32,'ep'=8] {'ep'}, dimensions={0} | all-to-all | bytes 4194304 | tf_op jit(solution)/shard_map/all_to_all | solution.py:219
  154.5 8.6 %experts.1 = bf16[512,2048]{1,0:T(8,128)(2,1)S(1)} custom-call(bf16[512,2048]{1,0:T(8,128)(2,1)S(1)} %bitcast.42, bf16[2048,768]{1,0:T(8,128)(2,1)} %bitcast.48, bf16[2048,768]{1,0:T(8,128)(2,1)} %bitcast.49, bf16[768,2048]{1,0:T(8,128)(2,1)} %bitcast.50), custom_call_target="tpu_custom_call" | custom-call | tf_op jit(solution)/shard_map/experts/pallas_call | solution.py:222
  163.1 1.3 copy-done
  164.5 4.7 %all-to-all-start.2 = ((bf16[8,64,2048]{2,1,0:T(8,128)(2,1)}), bf16[8,64,2048]{2,1,0:T(8,128)(2,1)S(1)}, u32[]{:S(2)}, u32[]{:S(2)}) async-start(bf16[8,64,2048]{2,1,0:T(8,128)(2,1)} %bitcast.41), calls=%async_computation.2 | async-start | bytes 4194304 | tf_op jit(solution)/shard_map/all_to_all | solution.py:236
  169.1 0.1 copy.28.target
  169.3 0.1 copy.27.gate_prob
  169.4 26.1 %all-to-all-done.2 = bf16[8,64,2048]{2,1,0:T(8,128)(2,1)S(1)} async-done(((bf16[8,64,2048]{2,1,0:T(8,128)(2,1)}), bf16[8,64,2048]{2,1,0:T(8,128)(2,1)S(1)}, u32[]{:S(2)}, u32[]{:S(2)}) %all-to-all-start.2) | async-done | bytes 2097184 | tf_op jit(solution)/shard_map/all_to_all | solution.py:236
  195.5 1.7 combine.1
  (21 shorter events, 0.1 us)
Async XLA Ops:
  6.5 105.7 %all-gather.2.cloned.1.call-start = ((), (), s32[]{:S(2)}) async-start(), calls=%async_computation.3 | async-start | bytes 8650752 | tf_op jit(solution)/shard_map/all_gather | solution.py:166
  9.2 14.5 %collective-permute-start = (bf16[256,512]{1,0:T(8,128)(2,1)S(1)}, bf16[256,512]{1,0:T(8,128)(2,1)S(1)}, u32[]{:S(2)}, u32[]{:S(2)}) collective-permute-start(bf16[256,512]{1,0:T(8,128)(2,1)S(1)} %pad_maximum_fusion.own), channel_id=1, source_target_pairs={{0,64},{8,72},{16,80},{24,88},{32,96},{40,104},{48,112},{56,120},{... | collective-permute-start | bytes 786440 | tf_op jit(solution)/shard_map/ppermute | solution.py:162
  25.4 9.1 %copy-start.8 = (s32[1,16]{1,0:T(1,128)S(1)}, s32[1,16]{1,0:T(1,128)}, u32[]{:S(2)}) copy-start(s32[1,16]{1,0:T(1,128)} %param.16) | copy-start | bytes 196
  25.4 13.0 %copy-start.6 = (s32[1,256,1]{1,2,0:T(1,128)S(1)}, s32[1,256,1]{1,2,0:T(1,128)}, u32[]{:S(2)}) copy-start(s32[1,256,1]{1,2,0:T(1,128)} %param.19) | copy-start | bytes 3076
  25.4 40.5 %all-to-all-start = ((bf16[8,256,512]{2,1,0:T(8,128)(2,1)}), bf16[8,256,512]{2,1,0:T(8,128)(2,1)S(1)}, u32[]{:S(2)}, u32[]{:S(2)}) async-start(bf16[8,256,512]{2,1,0:T(8,128)(2,1)} %broadcast_select_fusion), calls=%async_computation | async-start | bytes 4194304 | tf_op jit(solution)/shard_map/all_to_all | solution.py:165
  65.8 1.2 copy-start.4
  67.1 45.2 %copy-start.5 = (f32[2048]{0:T(1024)S(1)}, f32[2048]{0:T(1024)}, u32[]{:S(2)}) copy-start(f32[2048]{0:T(1024)} %param.18) | copy-start | bytes 24580
  112.2 1.2 copy-start.1
  121.9 1.0 copy-start.2
  163.1 1.4 copy-start
  164.5 4.8 %copy-start.7 = (f32[1,256,1]{1,2,0:T(1,128)S(1)}, f32[1,256,1]{1,2,0:T(1,128)}, u32[]{:S(2)}) copy-start(f32[1,256,1]{1,2,0:T(1,128)} %param.20) | copy-start | bytes 3076
  164.5 31.0 %copy-start.3 = (bf16[256,2048]{1,0:T(8,128)(2,1)S(1)}, bf16[256,2048]{1,0:T(8,128)(2,1)}, u32[]{:S(2)}) copy-start(bf16[256,2048]{1,0:T(8,128)(2,1)} %copy-done.2) | copy-start | bytes 3145732
  164.5 31.0 %all-to-all-start.2 = ((bf16[8,64,2048]{2,1,0:T(8,128)(2,1)}), bf16[8,64,2048]{2,1,0:T(8,128)(2,1)S(1)}, u32[]{:S(2)}, u32[]{:S(2)}) async-start(bf16[8,64,2048]{2,1,0:T(8,128)(2,1)} %bitcast.41), calls=%async_computation.2 | async-start | bytes 4194304 | tf_op jit(solution)/shard_map/all_to_all | solution.py:236
Sparse Core Ops, SparseCore 0:
  9.9 102.2 all-gather.1
